TPU v7x, 32 devices: a whole 2x2x4 slice. The times are simulated.
32 devices in a mesh: groups: 2 (over x), inp: 8 (over z, y), out: 2 (over core).
Axes of the slice: x: 2, y: 2, z: 4, core: 2. Of those that a mesh axis runs over, the one named last changes fastest.
Arguments:
- inputs: bfloat16 [1024, 4096], P(('groups', 'inp'), 'out'), parts along dimension 0, may hold values from -6 to 6
- pre_act: bfloat16 [1024, 12288], P('groups', 'inp'), parts along dimension 0, may hold values from -6 to 6
- out_grad: bfloat16 [1024, 4096], P(('groups', 'inp'), 'out'), parts along dimension 0, may hold values from -0.15625 to 0.15625
- w_down: bfloat16 [12288, 4096], P('inp', 'out'), may hold values from -0.0546875 to 0.0546875
- gram_state: float32 [4096, 2, 2048], P(('groups', 'inp'), 'out'), parts along dimension 0, may hold values from -6 to 6
Outputs:
- grad_down: bfloat16 [24576, 4096], P(('groups', 'inp'), 'out'), parts along dimension 0
- grad_up: bfloat16 [8192, 12288], P(('groups', 'out'), 'inp'), parts along dimension 0
- gram_new: float32 [4096, 2, 2048], P(('groups', 'inp'), 'out'), parts along dimension 0
There are 2 independent parts, one for each index of `groups`. A program takes and returns all parts, laid end to end along the dimension named above; an argument that names none is the same for every part. Nothing has to cross between parts.
All inputs are finite; a program needn't handle non-finite values.
Results may differ from a plain program's by a relative error of at most 0.008.
Values may be sent and summed in bfloat16 or wider, within the bound.
A program may use at most 128 MiB of HBM per device.

v0:
```python
import jax
import jax.numpy as jnp
from jax import lax
from jax.sharding import PartitionSpec as P

inv_root_two = 0.7071067811865476
inv_root_two_pi = 0.3989422804014327
ema_decay = 0.95


def gelu_pair(pre_float):
    normal_cdf = 0.5 * (1.0 + lax.erf(pre_float * inv_root_two))
    density = jnp.exp(-0.5 * pre_float * pre_float) * inv_root_two_pi
    return (pre_float * normal_cdf, normal_cdf + pre_float * density)


def over_rows(left, right):
    return lax.dot_general(
        left, right, (((0,), (0,)), ((), ())), preferred_element_type=jnp.float32
    )


def over_columns(left, right):
    return lax.dot_general(
        left, right, (((1,), (1,)), ((), ())), preferred_element_type=jnp.float32
    )


def shards(inputs, pre_act, out_grad, w_down, gram_state):
    gelu_value, gelu_slope = gelu_pair(pre_act.astype(jnp.float32))
    activation = gelu_value.astype(jnp.bfloat16)
    hidden_local = w_down.shape[0]
    portion = lax.all_gather(out_grad, "inp", axis=0, tiled=True)
    down_sum = over_rows(activation, portion)
    product = over_columns(portion, w_down)
    grad_down = down_sum.astype(jnp.bfloat16)
    act_grad = lax.psum(product, "out")
    hid_grad = (act_grad * gelu_slope).astype(jnp.bfloat16)
    up_total = over_rows(lax.all_gather(inputs, "inp", axis=0, tiled=True), hid_grad)
    grad_up = up_total.astype(jnp.bfloat16)
    block_count = gram_state.shape[1]
    block_size = gram_state.shape[2]
    blocks = grad_down.reshape(hidden_local, block_count, block_size)
    summed = lax.psum_scatter(
        jnp.einsum("fbj,fbc->jbc", blocks, blocks, preferred_element_type=jnp.float32).astype(
            jnp.bfloat16
        ),
        "inp",
        scatter_dimension=0,
        tiled=True,
    ).astype(jnp.float32)
    gram_new = ema_decay * gram_state + (1.0 - ema_decay) * summed
    return (grad_down, grad_up, gram_new)


def solution(mesh):
    return jax.shard_map(
        shards,
        mesh=mesh,
        in_specs=(
            P(("groups", "inp"), "out"),
            P("groups", "inp"),
            P(("groups", "inp"), "out"),
            P("inp", "out"),
            P(("groups", "inp"), "out", None),
        ),
        out_specs=(
            P(("groups", "inp"), "out"),
            P(("groups", "out"), "inp"),
            P(("groups", "inp"), "out", None),
        ),
        check_vma=False,
    )
```

profile of v0, /device:TPU:0, one launch (start us, length us, event | category | flops | bytes accessed | tf_op | source)
XLA Modules:
  0.0 306.7 jit_solution(6095876295094952623)
XLA Ops:
  7.2 0.0 all-gather.3.cloned.1.call-start
  7.2 0.7 all-gather.3.cloned.1.call-update
  7.9 0.0 all-gather.5.cloned.1.call-start
  7.9 0.7 all-gather.5.cloned.1.call-update
  8.6 0.0 all-reduce.2.cloned.1.call-start
  8.7 53.5 %all-gather.3.cloned.1.call-done = bf16[512,2048]{1,0:T(8,128)(2,1)} async-done(((bf16[64,2048]{1,0:T(8,128)(2,1)}), bf16[512,2048]{1,0:T(8,128)(2,1)}) %all-gather.3.cloned.1.call-update) | async-done | bytes 2097168 | tf_op jit(solution)/shard_map/all_gather | solution.py:33
  62.1 8.5 %fusion.18 = f32[512,1536]{1,0:T(8,128)} fusion(bf16[512,2048]{1,0:T(8,128)(2,1)} %all-gather.3.cloned.1.call-done, bf16[1536,2048]{1,0:T(8,128)(2,1)} %param.8), kind=kOutput, calls=%fused_computation.23 | convolution fusion | flops 3221225472 | bytes 11534336 | tf_op jit(solution)/shard_map/dot_general | solution.py:24
  70.7 0.0 copy-start
  70.7 0.0 all-reduce.2.cloned.1.call-update
  70.7 0.2 reduce-scatter.2.cloned.1.call-start
  70.9 1.4 copy-done
  72.4 5.0 %convolution_convert_fusion.1 = bf16[1536,2048]{1,0:T(8,128)(2,1)S(1)} fusion(bf16[512,2048]{1,0:T(8,128)(2,1)S(1)} %copy-done, bf16[512,1536]{1,0:T(8,128)(2,1)} %param.6), kind=kOutput, calls=%fused_computation.2 | convolution fusion | flops 3229089792 | bytes 9961472 | tf_op jit(solution)/shard_map/dot_general | solution.py:18
  77.3 0.0 copy-start.1
  77.3 2.7 copy-done.1
  80.0 15.4 %convert_bitcast_fusion = bf16[2048,1,2048]{0,2,1:T(8,128)(2,1)} fusion(bf16[1536,2048]{1,0:T(8,128)(2,1)S(1)} %convolution_convert_fusion.1), kind=kOutput, calls=%fused_computation | convolution fusion | flops 12889096192 | bytes 14680064 | tf_op jit(solution)/shard_map/fbj,fbc->jbc/dot_general | solution.py:45
  95.4 0.0 reduce-scatter.2.cloned.1.call-update
  95.4 4.6 %copy.8 = f32[256,1,2048]{0,2,1:T(8,128)S(1)} copy(f32[256,1,2048]{2,1,0:T(1,128)} %param.9) | data formatting | bytes 4194304 | tf_op args[4]
  100.0 12.1 %all-gather.5.cloned.1.call-done = bf16[512,2048]{1,0:T(8,128)(2,1)} async-done(((bf16[64,2048]{1,0:T(8,128)(2,1)}), bf16[512,2048]{1,0:T(8,128)(2,1)}) %all-gather.5.cloned.1.call-update) | async-done | bytes 2097168 | tf_op jit(solution)/shard_map/all_gather | solution.py:39
  112.1 24.7 %all-reduce.2.cloned.1.call-done = f32[512,1536]{1,0:T(8,128)} async-done(((f32[512,1536]{1,0:T(8,128)}), f32[512,1536]{1,0:T(8,128)}) %all-reduce.2.cloned.1.call-update) | async-done | bytes 3145744 | tf_op jit(solution)/shard_map/psum | solution.py:37
  136.7 10.2 %fusion = bf16[2048,1536]{0,1:T(8,128)(2,1)} fusion(bf16[512,2048]{1,0:T(8,128)(2,1)} %all-gather.5.cloned.1.call-done, f32[512,1536]{1,0:T(8,128)} %all-reduce.2.cloned.1.call-done, bf16[512,1536]{1,0:T(8,128)(2,1)} %param.6), kind=kOutput, calls=%fused_computation.3 | convolution fusion | flops 3233021952 | bytes 13107200 | tf_op jit(solution)/shard_map/dot_general | solution.py:18
  146.9 8.7 %copy.9 = bf16[2048,1536]{1,0:T(8,128)(2,1)} copy(bf16[2048,1536]{0,1:T(8,128)(2,1)} %fusion) | data formatting | bytes 12582912
  155.6 135.6 %reduce-scatter.2.cloned.1.call-done = bf16[256,1,2048]{0,2,1:T(8,128)(2,1)} async-done(((bf16[2048,1,2048]{0,2,1:T(8,128)(2,1)}), bf16[256,1,2048]{0,2,1:T(8,128)(2,1)}) %reduce-scatter.2.cloned.1.call-update) | async-done | bytes 1048592 | tf_op jit(solution)/shard_map/reduce_scatter | solution.py:44
  291.3 2.9 multiply_add_fusion
  294.1 6.0 %copy.10 = f32[256,1,2048]{2,1,0:T(1,128)} copy(f32[256,1,2048]{0,2,1:T(8,128)} %multiply_add_fusion) | data formatting | bytes 4194304
Async XLA Ops:
  7.2 55.0 %all-gather.3.cloned.1.call-start = ((), (), s32[]{:S(2)}) async-start(), calls=%async_computation.1 | async-start | bytes 2359296 | tf_op jit(solution)/shard_map/all_gather | solution.py:33
  7.9 104.2 %all-gather.5.cloned.1.call-start = ((), (), s32[]{:S(2)}) async-start(), calls=%async_computation.3 | async-start | bytes 2359296 | tf_op jit(solution)/shard_map/all_gather | solution.py:39
  8.6 128.1 %all-reduce.2.cloned.1.call-start = ((), (), s32[]{:S(2)}) async-start(), calls=%async_computation.2 | async-start | bytes 6291456 | tf_op jit(solution)/shard_map/psum | solution.py:37
  70.7 1.7 copy-start
  70.7 220.5 %reduce-scatter.2.cloned.1.call-start = ((), (), s32[]{:S(2)}) async-start(), calls=%async_computation.4 | async-start | bytes 9437184 | tf_op jit(solution)/shard_map/reduce_scatter | solution.py:44
  77.3 2.7 copy-start.1
Sparse Core Ops, SparseCore 0:
  10.1 51.9 all-gather.2
  64.3 47.7 all-gather.4
  115.0 21.6 all-reduce.1
  140.7 150.5 reduce-scatter.1
where the time goes:
time: 307 us
  waiting for transfers between devices  227 us (74%)
  matrix products  39.1 us (13%)
  local copies, waits for them, and re-layouts  23.4 us (8%)
  between operations  13.8 us (4%)
    reduce_scatter x1, waiting for transfers between devices, shards(): lax.psum_scatter(jnp.einsum('fbj,fbc->jbc', blocks, blocks, preferred_ele...  136 us
    all_gather x1, waiting for transfers between devices, shards(): portion = lax.all_gather(out_grad, 'inp', axis=0, tiled=True)  53.5 us
    psum x1, waiting for transfers between devices, shards(): act_grad = lax.psum(product, 'out')  24.7 us
    unnamed x7, local copies, waits for them, and re-layouts  23.4 us
    dot_general x1, matrix products, shards(): jnp.einsum('fbj,fbc->jbc', blocks, blocks, preferred_element_type=jnp.flo...  15.4 us
    dot_general x2, matrix products, over_rows(): lax.dot_general(left, right, (((0,), (0,)), ((), ())), preferred_element_...  15.2 us
    all_gather x1, waiting for transfers between devices, shards(): lax.all_gather(inputs, 'inp', axis=0, tiled=True)  12.1 us
    dot_general x1, matrix products, over_columns(): lax.dot_general(left, right, (((1,), (1,)), ((), ())), preferred_element_...  8.53 us
  transfers between devices with their start and end apart: 4, of which 4 were waited for; matrix products, arithmetic and copies ran while one was open for 17% of the time, Pallas kernels for 0%

commit v1 on v0

--- a/solution.py
+++ b/solution.py
@@ -26,30 +26,31 @@
     )
 
 
+def split_two(value):
+    high = value.astype(jnp.bfloat16)
+    return high, (value - high.astype(jnp.float32)).astype(jnp.bfloat16)
+
+
 def shards(inputs, pre_act, out_grad, w_down, gram_state):
     gelu_value, gelu_slope = gelu_pair(pre_act.astype(jnp.float32))
     activation = gelu_value.astype(jnp.bfloat16)
-    hidden_local = w_down.shape[0]
     portion = lax.all_gather(out_grad, "inp", axis=0, tiled=True)
+    token_gram = lax.psum(over_columns(activation, activation), "inp")
+    product = over_columns(portion, w_down)
+    act_grad = lax.psum(product, "out")
     down_sum = over_rows(activation, portion)
-    product = over_columns(portion, w_down)
     grad_down = down_sum.astype(jnp.bfloat16)
-    act_grad = lax.psum(product, "out")
     hid_grad = (act_grad * gelu_slope).astype(jnp.bfloat16)
     up_total = over_rows(lax.all_gather(inputs, "inp", axis=0, tiled=True), hid_grad)
     grad_up = up_total.astype(jnp.bfloat16)
-    block_count = gram_state.shape[1]
-    block_size = gram_state.shape[2]
-    blocks = grad_down.reshape(hidden_local, block_count, block_size)
-    summed = lax.psum_scatter(
-        jnp.einsum("fbj,fbc->jbc", blocks, blocks, preferred_element_type=jnp.float32).astype(
-            jnp.bfloat16
-        ),
-        "inp",
-        scatter_dimension=0,
-        tiled=True,
-    ).astype(jnp.float32)
-    gram_new = ema_decay * gram_state + (1.0 - ema_decay) * summed
+    rows = gram_state.shape[0]
+    own = lax.dynamic_slice_in_dim(portion, lax.axis_index("inp") * rows, rows, 1)
+    gram_high, gram_low = split_two(token_gram)
+    left_high, left_low = split_two(over_rows(own, gram_high) + over_rows(own, gram_low))
+    summed = jnp.dot(left_high, portion, preferred_element_type=jnp.float32) + jnp.dot(
+        left_low, portion, preferred_element_type=jnp.float32
+    )
+    gram_new = ema_decay * gram_state + (1.0 - ema_decay) * summed[:, None, :]
     return (grad_down, grad_up, gram_new)
 
 

time: 307 us -> 244 us (0.79)
  waiting for transfers between devices: 227 us -> 184 us
  local copies, waits for them, and re-layouts: 23.4 us -> 12.1 us
  matrix products: 39.1 us -> 34.3 us
    reduce_scatter x1 -> x0, waiting for transfers between devices: 136 us -> none  [shards(): lax.psum_scatter(jnp.einsum('fbj,fbc->jbc', blocks, blocks, preferred_ele...]
    psum x0 -> x1, waiting for transfers between devices: none -> 72 us  [shards(): token_gram = lax.psum(over_columns(activation, activation), 'inp')]
    all_gather x1, waiting for transfers between devices: 12.1 us -> 36.7 us  [shards(): lax.all_gather(inputs, 'inp', axis=0, tiled=True)]
    dot_general x1 -> x2, matrix products: 15.4 us -> 2.08 us  [the longest x1 1.36 us: shards(): jnp.dot(left_low, portion, preferred_element_type=jnp.float32)]
    unnamed x7 -> x8, local copies, waits for them, and re-layouts: 23.4 us -> 12.1 us
    all_gather x1, waiting for transfers between devices: 53.5 us -> 49 us  [shards(): portion = lax.all_gather(out_grad, 'inp', axis=0, tiled=True)]
    dot_general x1 -> x2, matrix products: 8.53 us -> 13 us  [over_columns(): lax.dot_general(left, right, (((1,), (1,)), ((), ())), preferred_element_...]
    dot_general x2 -> x4, matrix products: 15.2 us -> 19.2 us  [over_rows(): lax.dot_general(left, right, (((0,), (0,)), ((), ())), preferred_element_...]
  transfers between devices with their start and end apart: 4 -> 4, of which waited for: 4 -> 4; matrix products, arithmetic and copies ran while one was open for 17% -> 11% of each run, Pallas kernels for 0% -> 0%
where the time goes in v1:
time: 244 us
  waiting for transfers between devices  184 us (75%)
  matrix products  34.3 us (14%)
  between operations  13.8 us (6%)
  local copies, waits for them, and re-layouts  12.1 us (5%)
    psum x1, waiting for transfers between devices, shards(): token_gram = lax.psum(over_columns(activation, activation), 'inp')  72 us
    all_gather x1, waiting for transfers between devices, shards(): portion = lax.all_gather(out_grad, 'inp', axis=0, tiled=True)  49 us
    all_gather x1, waiting for transfers between devices, shards(): lax.all_gather(inputs, 'inp', axis=0, tiled=True)  36.7 us
    psum x1, waiting for transfers between devices, shards(): act_grad = lax.psum(product, 'out')  24.6 us
    dot_general x4, matrix products, over_rows(): lax.dot_general(left, right, (((0,), (0,)), ((), ())), preferred_element_...  19.2 us
    dot_general x2, matrix products, over_columns(): lax.dot_general(left, right, (((1,), (1,)), ((), ())), preferred_element_...  13 us
    unnamed x8, local copies, waits for them, and re-layouts  12.1 us
  transfers between devices with their start and end apart: 4, of which 4 were waited for; matrix products, arithmetic and copies ran while one was open for 11% of the time, Pallas kernels for 0%

profile of v1, /device:TPU:0, one launch (start us, length us, event | category | flops | bytes accessed | tf_op | source)
XLA Modules:
  0.0 243.9 jit_solution(8409857993915918993)
XLA Ops:
  7.2 0.0 all-gather.3.cloned.1.call-start
  7.2 0.7 all-gather.3.cloned.1.call-update
  7.9 0.0 all-reduce.5.cloned.1.call-start
  7.9 4.4 %fusion.28 = f32[512,512]{1,0:T(8,128)} fusion(bf16[512,1536]{1,0:T(8,128)(2,1)} %param.6), kind=kOutput, calls=%fused_computation.39 | convolution fusion | flops 810024960 | bytes 2621440 | tf_op jit(solution)/shard_map/dot_general | solution.py:24
  12.4 0.0 all-reduce.5.cloned.1.call-update
  12.4 0.0 all-gather.5.cloned.1.call-start
  12.5 0.7 all-gather.5.cloned.1.call-update
  13.1 0.0 all-reduce.3.cloned.1.call-start
  13.2 49.0 %all-gather.3.cloned.1.call-done = bf16[512,2048]{1,0:T(8,128)(2,1)} async-done(((bf16[64,2048]{1,0:T(8,128)(2,1)}), bf16[512,2048]{1,0:T(8,128)(2,1)}) %all-gather.3.cloned.1.call-update) | async-done | bytes 2097168 | tf_op jit(solution)/shard_map/all_gather | solution.py:37
  62.1 8.5 %fusion.34 = f32[512,1536]{1,0:T(8,128)} fusion(bf16[512,2048]{1,0:T(8,128)(2,1)} %all-gather.3.cloned.1.call-done, bf16[1536,2048]{1,0:T(8,128)(2,1)} %param.8), kind=kOutput, calls=%fused_computation.40 | convolution fusion | flops 3221225472 | bytes 11534336 | tf_op jit(solution)/shard_map/dot_general | solution.py:24
  70.7 0.0 copy-start
  70.7 0.0 all-reduce.3.cloned.1.call-update
  70.7 72.0 %all-reduce.5.cloned.1.call-done = f32[512,512]{1,0:T(8,128)} async-done(((f32[512,512]{1,0:T(8,128)}), f32[512,512]{1,0:T(8,128)}) %all-reduce.5.cloned.1.call-update) | async-done | bytes 1048592 | tf_op jit(solution)/shard_map/psum | solution.py:38
  142.7 0.0 copy-done
  142.7 1.5 fusion.17
  144.3 0.0 copy-start.1
  144.3 2.0 convolution_add_fusion.1
  146.3 0.7 fusion.22
  147.1 0.0 copy-done.1
  147.1 1.4 fusion.12
  148.4 0.0 copy-start.2
  148.4 3.5 %copy.10 = f32[256,1,2048]{2,1,0:T(1,128)} copy(f32[256,1,2048]{2,0,1:T(8,128)S(1)} %fusion.12) | data formatting | bytes 4194304
  151.9 0.0 copy-done.2
  151.9 5.4 %convolution_convert_fusion.1 = bf16[1536,2048]{1,0:T(8,128)(2,1)} fusion(bf16[512,2048]{1,0:T(8,128)(2,1)S(1)} %copy-done, bf16[512,1536]{1,0:T(8,128)(2,1)S(1)} %copy-done.2), kind=kOutput, calls=%fused_computation.1 | convolution fusion | flops 3229089792 | bytes 9961472 | tf_op jit(solution)/shard_map/dot_general | solution.py:18
  157.3 36.7 %all-gather.5.cloned.1.call-done = bf16[512,2048]{1,0:T(8,128)(2,1)} async-done(((bf16[64,2048]{1,0:T(8,128)(2,1)}), bf16[512,2048]{1,0:T(8,128)(2,1)}) %all-gather.5.cloned.1.call-update) | async-done | bytes 2097168 | tf_op jit(solution)/shard_map/all_gather | solution.py:44
  194.0 24.6 %all-reduce.3.cloned.1.call-done = f32[512,1536]{1,0:T(8,128)} async-done(((f32[512,1536]{1,0:T(8,128)}), f32[512,1536]{1,0:T(8,128)}) %all-reduce.3.cloned.1.call-update) | async-done | bytes 3145744 | tf_op jit(solution)/shard_map/psum | solution.py:40
  218.6 10.2 %fusion = bf16[2048,1536]{0,1:T(8,128)(2,1)} fusion(bf16[512,2048]{1,0:T(8,128)(2,1)} %all-gather.5.cloned.1.call-done, f32[512,1536]{1,0:T(8,128)} %all-reduce.3.cloned.1.call-done, bf16[512,1536]{1,0:T(8,128)(2,1)} %param.6), kind=kOutput, calls=%fused_computation.2 | convolution fusion | flops 3233021952 | bytes 13107200 | tf_op jit(solution)/shard_map/dot_general | solution.py:18
  228.8 8.6 %copy.9 = bf16[2048,1536]{1,0:T(8,128)(2,1)} copy(bf16[2048,1536]{0,1:T(8,128)(2,1)} %fusion) | data formatting | bytes 12582912
Async XLA Ops:
  7.2 55.0 %all-gather.3.cloned.1.call-start = ((), (), s32[]{:S(2)}) async-start(), calls=%async_computation | async-start | bytes 2359296 | tf_op jit(solution)/shard_map/all_gather | solution.py:37
  7.9 134.8 %all-reduce.5.cloned.1.call-start = ((), (), s32[]{:S(2)}) async-start(), calls=%async_computation.3 | async-start | bytes 2097152 | tf_op jit(solution)/shard_map/psum | solution.py:38
  12.4 181.6 %all-gather.5.cloned.1.call-start = ((), (), s32[]{:S(2)}) async-start(), calls=%async_computation.2 | async-start | bytes 2359296 | tf_op jit(solution)/shard_map/all_gather | solution.py:44
  13.1 205.4 %all-reduce.3.cloned.1.call-start = ((), (), s32[]{:S(2)}) async-start(), calls=%async_computation.1 | async-start | bytes 6291456 | tf_op jit(solution)/shard_map/psum | solution.py:40
  70.7 72.0 %copy-start = (bf16[512,2048]{1,0:T(8,128)(2,1)S(1)}, bf16[512,2048]{1,0:T(8,128)(2,1)}, u32[]{:S(2)}) copy-start(bf16[512,2048]{1,0:T(8,128)(2,1)} %all-gather.3.cloned.1.call-done) | copy-start | bytes 6291460
  144.3 2.8 %copy-start.1 = (f32[256,1,2048]{2,1,0:T(1,128)S(1)}, f32[256,1,2048]{2,1,0:T(1,128)}, u32[]{:S(2)}) copy-start(f32[256,1,2048]{2,1,0:T(1,128)} %param.9) | copy-start | bytes 6291460
  148.4 3.5 %copy-start.2 = (bf16[512,1536]{1,0:T(8,128)(2,1)S(1)}, bf16[512,1536]{1,0:T(8,128)(2,1)}, u32[]{:S(2)}) copy-start(bf16[512,1536]{1,0:T(8,128)(2,1)} %param.6) | copy-start | bytes 4718596
Sparse Core Ops, SparseCore 0:
  10.1 51.9 all-gather.2
  66.2 76.4 all-reduce.4
  145.1 48.8 all-gather.4
  196.9 21.6 all-reduce.2

commit v2 on v1

v2 whole, which is shorter than its diff:
```python
import functools

import jax
import jax.numpy as jnp
from jax import lax
from jax.experimental import pallas as pl
from jax.experimental.pallas import tpu as pltpu
from jax.sharding import PartitionSpec as P

inv_root_two = 0.7071067811865476
inv_root_two_pi = 0.3989422804014327
ema_decay = 0.95
MESH = pl.DeviceIdType.MESH
BF16 = jnp.bfloat16
F32 = jnp.float32
CHUNKS = 4


def gelu_pair(pre_float):
    normal_cdf = 0.5 * (1.0 + lax.erf(pre_float * inv_root_two))
    density = jnp.exp(-0.5 * pre_float * pre_float) * inv_root_two_pi
    return (pre_float * normal_cdf, normal_cdf + pre_float * density)


def nt(left, right):
    return lax.dot_general(left, right, (((1,), (1,)), ((), ())), preferred_element_type=F32)


def tn(left, right):
    return lax.dot_general(left, right, (((0,), (0,)), ((), ())), preferred_element_type=F32)


def nn(left, right):
    return jnp.dot(left, right, preferred_element_type=F32)


def exchange(
    n,
    inputs,
    pre_act,
    out_grad,
    w_down,
    o_full,
    i_full,
    hid_out,
    act_out,
    s_out,
    o_v,
    pre_v,
    act_v,
    act_t,
    w_v,
    slope_v,
    own_v,
    part_send,
    part_recv,
    hid_v,
    s1_keep,
    s1_send,
    s1_recv,
    s2_send,
    s2_recv,
    s_v,
    ring_send,
    ring_recv,
    part_ssem,
    part_rsem,
    s1_sem,
    s2_ssem,
    s2_rsem,
    s3_ssem,
    s3_rsem,
    s4_sem,
    s5_sem,
    pre_sem,
    local_sem,
):
    grp, idx, core = lax.axis_index("groups"), lax.axis_index("inp"), lax.axis_index("out")
    ts, width = out_grad.shape
    tokens, hidden = pre_act.shape
    half_rows = ts // 2
    A = n // 2
    a, b = lax.div(idx, 2), lax.rem(idx, 2)
    hops = n // 2
    folded = n <= 8

    def at(p):
        p = lax.rem(p + 2 * n, n)
        if not folded:
            return p
        q = lax.div(p, A)
        return (1 - q) * (2 * p) + q * (2 * (n - 1 - p) + 1)

    pos = a * (1 - b) + (n - 1 - a) * b if folded else idx

    def slot(i):
        return lax.rem(i, 2) * A + lax.div(i, 2)

    def dev(i, c=core):
        return (grp, i, c)

    barrier = pltpu.get_barrier_semaphore()
    for d in range(1, n):
        pl.semaphore_signal(barrier, inc=1, device_id=dev(lax.rem(idx + d, n)), device_id_type=MESH)
    pl.semaphore_signal(barrier, inc=1, device_id=dev(idx, 1 - core), device_id_type=MESH)

    w_copy = pltpu.make_async_copy(w_down, w_v, local_sem.at[0])
    w_copy.start()
    pre_copies = []
    for j in range(n):
        copy = pltpu.make_async_copy(
            pre_act.at[pl.ds(j * ts, ts)], pre_v.at[pl.ds(((j % 2) * A + j // 2) * ts, ts)], pre_sem.at[j]
        )
        copy.start()
        pre_copies.append(copy)
    own_rows = pl.ds(pl.multiple_of(slot(idx) * ts, ts), ts)
    o_own = pltpu.make_async_copy(out_grad, o_v.at[own_rows], local_sem.at[1])
    o_own.start()
    i_own = pltpu.make_async_copy(inputs, i_full.at[own_rows], local_sem.at[2])
    i_own.start()
    pl.semaphore_wait(barrier, n)

    arrays = ((out_grad, o_v), (inputs, i_full))

    def exists(way, h, half):
        return h < hops or half == way

    def message(arr, way, h, half):
        sign = 1 - 2 * way
        mine, full = arrays[arr]
        place = slot(at(pos - sign * (h - 1)))
        rows = pl.ds(pl.multiple_of(place * ts + half * half_rows, half_rows), half_rows)
        src = mine.at[pl.ds(half * half_rows, half_rows)] if h == 1 else full.at[rows]
        return pltpu.make_async_remote_copy(
            src_ref=src,
            dst_ref=full.at[rows],
            send_sem=ring_send.at[arr, way, h - 1, half],
            recv_sem=ring_recv.at[arr, way, h - 1, half],
            device_id=dev(at(pos + sign)),
            device_id_type=MESH,
        )

    def arrived(arr, way, h, half):
        sign = 1 - 2 * way
        full = arrays[arr][1]
        place = slot(at(pos - sign * h))
        rows = pl.ds(pl.multiple_of(place * ts + half * half_rows, half_rows), half_rows)
        return pltpu.make_async_remote_copy(
            src_ref=full.at[rows],
            dst_ref=full.at[rows],
            send_sem=ring_send.at[arr, way, h - 1, half],
            recv_sem=ring_recv.at[arr, way, h - 1, half],
            device_id=dev(at(pos + sign)),
            device_id_type=MESH,
        )

    sent = []

    def push(arr, h, half, ways=(0, 1)):
        for way in ways:
            if exists(way, h, half):
                copy = message(arr, way, h, half)
                copy.start()
                sent.append(copy)

    def tick(arr, h, half):
        for way in (0, 1):
            if exists(way, h, half):
                arrived(arr, way, h, half).wait_recv()
                if h < hops:
                    push(arr, h + 1, half, (way,))

    for half in (0, 1):
        push(0, 1, half)

    ticks = [(h, half) for h in range(1, hops + 1) for half in (0, 1)]
    col = 256 if hidden % 256 == 0 else 128
    gelu_rows = 32

    def gelu_part(j):
        pre_copies[(j // A) + 2 * (j % A)].wait()

        @pl.loop(0, ts // gelu_rows)
        def _(r):
            rows = pl.ds(pl.multiple_of(j * ts + r * gelu_rows, gelu_rows), gelu_rows)

            @pl.loop(0, hidden // col)
            def _(c):
                cols = pl.ds(pl.multiple_of(c * col, col), col)
                value, slope = gelu_pair(pre_v[rows, cols].astype(F32))
                act_v[rows, cols] = value.astype(BF16)
                slope_v[rows, cols] = slope

    for k, (h, half) in enumerate(ticks):
        if k < n:
            gelu_part(k)
        tick(0, h, half)
        if (h, half) == (max(hops - 2, 1), 1):
            for other in (0, 1):
                push(1, 1, other)
    for k in range(len(ticks), n):
        gelu_part(k)
    o_own.wait()
    o_store = pltpu.make_async_copy(o_v, o_full, local_sem.at[1])
    o_store.start()

    span = tokens // 2
    core_cols = pl.ds(pl.multiple_of(core * span, span), span)
    partner = 2 * a + 1 - b
    group_rows = A * ts

    def s_rows(parity, keep):
        @pl.loop(0, A)
        def _(k):
            rows = pl.ds(pl.multiple_of(parity * group_rows + k * ts, ts), ts)
            value = nt(act_v[rows, :], act_v[core_cols, :])
            if keep:
                s1_keep[k] = value
            else:
                s1_send[k] = value.astype(BF16)

    s_rows(1 - b, False)
    s1 = pltpu.make_async_remote_copy(
        src_ref=s1_send,
        dst_ref=s1_recv,
        send_sem=s1_sem.at[0],
        recv_sem=s1_sem.at[1],
        device_id=dev(partner),
        device_id_type=MESH,
    )
    s1.start()
    s_rows(b, True)

    i_ticks = list(ticks)

    def next_tick():
        if i_ticks:
            tick(1, *i_ticks.pop(0))

    w_copy.wait()
    part_rows = tokens // CHUNKS
    part_copies = []
    for k in range(CHUNKS):
        rows = pl.ds(k * part_rows, part_rows)
        wcol = 512 if hidden % 512 == 0 else 128

        @pl.loop(0, hidden // wcol)
        def _(c):
            cols = pl.ds(pl.multiple_of(c * wcol, wcol), wcol)
            value = nt(o_v[rows, :], w_v[cols, :])
            own_v[rows, cols] = value
            part_send[rows, cols] = value.astype(BF16)

        copy = pltpu.make_async_remote_copy(
            src_ref=part_send.at[rows],
            dst_ref=part_recv.at[rows],
            send_sem=part_ssem.at[k],
            recv_sem=part_rsem.at[k],
            device_id=dev(idx, 1 - core),
            device_id_type=MESH,
        )
        copy.start()
        part_copies.append(copy)
        next_tick()

    s1.wait()

    @pl.loop(0, A)
    def _(k):
        value = s1_keep[k] + s1_recv[k].astype(F32)
        s1_keep[k] = value
        s2_send[k] = value.astype(BF16)

    s2_copies = []
    for d in range(1, A):
        there = lax.rem(a + d, A)
        copy = pltpu.make_async_remote_copy(
            src_ref=s2_send.at[there],
            dst_ref=s2_recv.at[d - 1],
            send_sem=s2_ssem.at[d - 1],
            recv_sem=s2_rsem.at[d - 1],
            device_id=dev(2 * there + b),
            device_id_type=MESH,
        )
        copy.start()
        s2_copies.append(copy)

    for k in range(CHUNKS):
        part_copies[k].wait_recv()

        @pl.loop(0, part_rows // gelu_rows)
        def _(r):
            rows = pl.ds(pl.multiple_of(k * part_rows + r * gelu_rows, gelu_rows), gelu_rows)

            @pl.loop(0, hidden // col)
            def _(c):
                cols = pl.ds(pl.multiple_of(c * col, col), col)
                total = own_v[rows, cols] + part_recv[rows, cols].astype(F32)
                hid_v[rows, cols] = (total * slope_v[rows, cols]).astype(BF16)

        if k % 2 == 1:
            next_tick()
    hid_store = pltpu.make_async_copy(hid_v, hid_out, local_sem.at[3])
    hid_store.start()

    for copy in s2_copies:
        copy.wait()
    total = s1_keep[a]
    for d in range(A - 1):
        total = total + s2_recv[d].astype(F32)
    s_v[core, b, a] = total.astype(BF16)
    s3_copies = []
    for d in range(1, A):
        there = lax.rem(a + d, A)
        copy = pltpu.make_async_remote_copy(
            src_ref=s_v.at[core, b, a],
            dst_ref=s_v.at[core, b, a],
            send_sem=s3_ssem.at[d - 1],
            recv_sem=s3_rsem.at[d - 1],
            device_id=dev(2 * there + b),
            device_id_type=MESH,
        )
        copy.start()
        s3_copies.append(copy)

    @pl.loop(0, hidden // 128)
    def _(c):
        block = pl.ds(pl.multiple_of(c * 128, 128), 128)
        act_t[block, :] = act_v[:, block].T

    act_store = pltpu.make_async_copy(act_t, act_out, local_sem.at[0])
    act_store.start()
    for d in range(1, A):
        copy = s3_copies[d - 1]
        copy.wait_send()
        back = lax.rem(a - d + A, A)
        pltpu.make_async_remote_copy(
            src_ref=s_v.at[core, b, back],
            dst_ref=s_v.at[core, b, back],
            send_sem=s3_ssem.at[d - 1],
            recv_sem=s3_rsem.at[d - 1],
            device_id=dev(2 * back + b),
            device_id_type=MESH,
        ).wait_recv()

    def swap(mine, theirs, sems, device):
        copy = pltpu.make_async_remote_copy(
            src_ref=s_v.at[mine],
            dst_ref=s_v.at[mine],
            send_sem=sems.at[0],
            recv_sem=sems.at[1],
            device_id=device,
            device_id_type=MESH,
        )
        copy.start()
        back = pltpu.make_async_remote_copy(
            src_ref=s_v.at[theirs],
            dst_ref=s_v.at[theirs],
            send_sem=sems.at[0],
            recv_sem=sems.at[1],
            device_id=device,
            device_id_type=MESH,
        )
        return copy, back

    copy, back = swap((core, b), (core, 1 - b), s4_sem, dev(partner))
    next_tick()
    copy.wait_send()
    back.wait_recv()
    copy, back = swap((core,), (1 - core,), s5_sem, dev(idx, 1 - core))
    while i_ticks:
        next_tick()
    copy.wait_send()
    back.wait_recv()
    s_store = pltpu.make_async_copy(s_v, s_out, local_sem.at[4])
    s_store.start()
    for copy in sent:
        copy.wait_send()
    for copy in part_copies:
        copy.wait_send()
    i_own.wait()
    o_store.wait()
    hid_store.wait()
    act_store.wait()
    s_store.wait()


def finish(act_t, hid, o_tile, i_tile, own, s, state, down, up, gram, left, s_keep, g_keep, sem):
    step = pl.program_id(0)
    rows = own.shape[1]
    tile = o_tile.shape[1]
    cols = pl.ds(pl.multiple_of(step * tile, tile), tile)

    @pl.when(step == 0)
    def _():
        copy = pltpu.make_async_copy(state.at[:, 0, :], s_keep, sem.at[0])
        copy.start()
        span = s.shape[2]
        for c in range(2):
            value = tn(own[...], s[c])
            high = value.astype(BF16)
            left[0, :, c * span : (c + 1) * span] = high
            left[1, :, c * span : (c + 1) * span] = (value - high.astype(F32)).astype(BF16)
        copy.wait()

    down[...] = nn(act_t[...], o_tile[...]).astype(BF16)
    up[...] = tn(i_tile[...], hid[...]).astype(BF16)
    total = nn(left[0], o_tile[...]) + nn(left[1], o_tile[...])
    g_keep[:, cols] = ema_decay * s_keep[:, cols] + (1.0 - ema_decay) * total

    @pl.when(step == pl.num_programs(0) - 1)
    def _():
        copy = pltpu.make_async_copy(g_keep, gram.at[:, 0, :], sem.at[1])
        copy.start()
        copy.wait()


def shards(n, inputs, pre_act, out_grad, w_down, gram_state):
    ts, width = out_grad.shape
    tokens, hidden = pre_act.shape
    A = n // 2
    span = tokens // 2
    hops = n // 2
    shape = jax.ShapeDtypeStruct
    dma = pltpu.SemaphoreType.DMA
    any_spec = pl.BlockSpec(memory_space=pl.ANY)
    vmem_spec = pl.BlockSpec(memory_space=pltpu.VMEM)
    extra = max(A - 1, 1)
    o_full, i_full, hid, act_t, s = pl.pallas_call(
        functools.partial(exchange, n),
        out_shape=(
            shape((tokens, width), BF16),
            shape((tokens, width), BF16),
            shape((tokens, hidden), BF16),
            shape((hidden, tokens), BF16),
            shape((2, 2, A, ts, span), BF16),
        ),
        in_specs=[any_spec, any_spec, vmem_spec, any_spec],
        out_specs=(any_spec,) * 5,
        scratch_shapes=[
            pltpu.VMEM((tokens, width), BF16),
            pltpu.VMEM((tokens, hidden), BF16),
            pltpu.VMEM((tokens, hidden), BF16),
            pltpu.VMEM((hidden, tokens), BF16),
            pltpu.VMEM((hidden, width), BF16),
            pltpu.VMEM((tokens, hidden), F32),
            pltpu.VMEM((tokens, hidden), F32),
            pltpu.VMEM((tokens, hidden), BF16),
            pltpu.VMEM((tokens, hidden), BF16),
            pltpu.VMEM((tokens, hidden), BF16),
            pltpu.VMEM((A, ts, span), F32),
            pltpu.VMEM((A, ts, span), BF16),
            pltpu.VMEM((A, ts, span), BF16),
            pltpu.VMEM((A, ts, span), BF16),
            pltpu.VMEM((extra, ts, span), BF16),
            pltpu.VMEM((2, 2, A, ts, span), BF16),
            dma((2, 2, hops, 2)),
            dma((2, 2, hops, 2)),
            dma((CHUNKS,)),
            dma((CHUNKS,)),
            dma((2,)),
            dma((extra,)),
            dma((extra,)),
            dma((extra,)),
            dma((extra,)),
            dma((2,)),
            dma((2,)),
            dma((n,)),
            dma((5,)),
        ],
        compiler_params=pltpu.CompilerParams(
            collective_id=0, has_side_effects=True, vmem_limit_bytes=56 * 1024 * 1024
        ),
        name="exchange",
    )(inputs, pre_act, out_grad, w_down)
    s = s.reshape(2, tokens, span)
    rows = gram_state.shape[0]
    own = lax.dynamic_slice_in_dim(o_full, lax.axis_index("inp") * rows, rows, 1)
    tile = 256
    keep = lambda i: (0, 0)
    return pl.pallas_call(
        finish,
        grid=(width // tile,),
        out_shape=(
            shape((hidden, width), BF16),
            shape((width, hidden), BF16),
            shape(gram_state.shape, F32),
        ),
        in_specs=[
            pl.BlockSpec((hidden, tokens), keep),
            pl.BlockSpec((tokens, hidden), keep),
            pl.BlockSpec((tokens, tile), lambda i: (0, i)),
            pl.BlockSpec((tokens, tile), lambda i: (0, i)),
            pl.BlockSpec((tokens, rows), keep),
            pl.BlockSpec((2, tokens, span), lambda i: (0, 0, 0)),
            any_spec,
        ],
        out_specs=(
            pl.BlockSpec((hidden, tile), lambda i: (0, i)),
            pl.BlockSpec((tile, hidden), lambda i: (i, 0)),
            any_spec,
        ),
        scratch_shapes=[
            pltpu.VMEM((2, rows, tokens), BF16),
            pltpu.VMEM((rows, width), F32),
            pltpu.VMEM((rows, width), F32),
            dma((2,)),
        ],
        compiler_params=pltpu.CompilerParams(vmem_limit_bytes=56 * 1024 * 1024),
        name="finish",
    )(act_t, hid, o_full, i_full, own, s, gram_state)


def solution(mesh):
    return jax.shard_map(
        functools.partial(shards, mesh.shape["inp"]),
        mesh=mesh,
        in_specs=(
            P(("groups", "inp"), "out"),
            P("groups", "inp"),
            P(("groups", "inp"), "out"),
            P("inp", "out"),
            P(("groups", "inp"), "out", None),
        ),
        out_specs=(
            P(("groups", "inp"), "out"),
            P(("groups", "out"), "inp"),
            P(("groups", "inp"), "out", None),
        ),
        check_vma=False,
    )
```

time: 244 us -> 85.6 us (0.35)
  waiting for transfers between devices: 184 us -> 0 us
  Pallas kernels: 0 us -> 82.8 us
  matrix products: 34.3 us -> 0 us
  between operations: 13.8 us -> 0.64 us
  local copies, waits for them, and re-layouts: 12.1 us -> 1.68 us
    psum x2 -> x0, waiting for transfers between devices: 96.6 us -> none  [the longest x1 72 us: shards(): token_gram = lax.psum(over_columns(activation, activation), 'inp')]
    all_gather x2 -> x0, waiting for transfers between devices: 85.6 us -> none  [the longest x1 49 us: shards(): portion = lax.all_gather(out_grad, 'inp', axis=0, tiled=True)]
    pallas_call x0 -> x2, Pallas kernels: none -> 82.8 us  [the longest x1 66.2 us: shards(): pl.pallas_call(functools.partial(exchange, n), out_shape=(shape((tokens,...]
    dot_general x8 -> x0, matrix products: 34.3 us -> none  [the longest x4 19.2 us: over_rows(): lax.dot_general(left, right, (((0,), (0,)), ((), ())), preferred_element_...]
    unnamed x8 -> x0, local copies, waits for them, and re-layouts: 12.1 us -> none
  transfers between devices with their start and end apart: 4 -> 0, of which waited for: 4 -> 0; matrix products, arithmetic and copies ran while one was open for 11% -> 0% of each run, Pallas kernels for 0% -> 0%
where the time goes in v2:
time: 85.6 us; the launch traced here: 85.1 us
  Pallas kernels  82.8 us (97%)
  local copies, waits for them, and re-layouts  1.68 us (2%)
    pallas_call x1, Pallas kernels, shards(): pl.pallas_call(functools.partial(exchange, n), out_shape=(shape((tokens,...  66.2 us
    pallas_call x1, Pallas kernels, shards(): pl.pallas_call(finish, grid=(width // tile,), out_shape=(shape((hidden, w...  16.6 us

profile of v2, /device:TPU:0, one launch (start us, length us, event | category | flops | bytes accessed | tf_op | source)
XLA Modules:
  0.0 85.1 jit_solution(15314329519061211963)
XLA Ops:
  0.6 66.2 %exchange.1 = (bf16[512,2048]{1,0:T(8,128)(2,1)}, bf16[512,2048]{1,0:T(8,128)(2,1)}, bf16[512,1536]{1,0:T(8,128)(2,1)}, bf16[1536,512]{1,0:T(8,128)(2,1)}, bf16[2,2,4,64,256]{4,3,2,1,0:T(8,128)(2,1)}) custom-call(bf16[64,2048]{1,0:T(8,128)(2,1)} %inputs.1, bf16[512,1536]{1,0:T(8,128)(2,1)} %pre_act.1, bf16[64,2048]{1,0:T(8,128)(2,1)} %out_grad.1, ...), custom_call_target="tpu_custom_call" | custom-call | tf_op jit(solution)/shard_map/exchange/pallas_call | solution.py:429
  66.9 1.7 %constant_dynamic-slice_fusion.own = bf16[512,256]{1,0:T(8,128)(2,1)} fusion(bf16[512,2048]{1,0:T(8,128)(2,1)} %get-tuple-element.10.o_tile, s32[]{:T(128)S(6)} %select_n.3), kind=kLoop, calls=%fused_computation | loop fusion | bytes 524292 | tf_op jit(solution)/shard_map/dynamic_slice | solution.py:478
  68.6 16.6 %finish.1 = (bf16[1536,2048]{1,0:T(8,128)(2,1)}, bf16[2048,1536]{1,0:T(8,128)(2,1)}, f32[256,1,2048]{2,1,0:T(1,128)}) custom-call(bf16[1536,512]{1,0:T(8,128)(2,1)} %get-tuple-element.8.act_t, bf16[512,1536]{1,0:T(8,128)(2,1)} %get-tuple-element.9.hid, bf16[512,2048]{1,0:T(8,128)(2,1)} %get-tuple-element.10.o_tile, ...), custom_call_target="tpu_custom_call" | custom-call | tf_op jit(solution)/shard_map/finish/pallas_call | solution.py:481

commit v3 on v2

--- a/solution.py
+++ b/solution.py
@@ -12,8 +12,8 @@
 ema_decay = 0.95
 MESH = pl.DeviceIdType.MESH
 BF16 = jnp.bfloat16
+STEPS = 4
 F32 = jnp.float32
-CHUNKS = 4
 
 
 def gelu_pair(pre_float):
@@ -73,6 +73,7 @@
     s4_sem,
     s5_sem,
     pre_sem,
+    hid_sem,
     local_sem,
 ):
     grp, idx, core = lax.axis_index("groups"), lax.axis_index("inp"), lax.axis_index("out")
@@ -172,8 +173,12 @@
 
     for half in (0, 1):
         push(0, 1, half)
-
-    ticks = [(h, half) for h in range(1, hops + 1) for half in (0, 1)]
+        push(1, 1, half)
+
+    def step(arr, h):
+        for half in (0, 1):
+            tick(arr, h, half)
+
     col = 256 if hidden % 256 == 0 else 128
     gelu_rows = 32
 
@@ -191,18 +196,64 @@
                 act_v[rows, cols] = value.astype(BF16)
                 slope_v[rows, cols] = slope
 
-    for k, (h, half) in enumerate(ticks):
-        if k < n:
-            gelu_part(k)
-        tick(0, h, half)
-        if (h, half) == (max(hops - 2, 1), 1):
-            for other in (0, 1):
-                push(1, 1, other)
-    for k in range(len(ticks), n):
-        gelu_part(k)
-    o_own.wait()
-    o_store = pltpu.make_async_copy(o_v, o_full, local_sem.at[1])
-    o_store.start()
+    part_copies = []
+
+    def shards_of(h):
+        if h == 0:
+            return [slot(idx)]
+        if h == hops:
+            return [slot(at(pos + h))]
+        return [slot(at(pos - h)), slot(at(pos + h))]
+
+    wcol = 512 if hidden % 512 == 0 else 128
+
+    def part(h):
+        for place in shards_of(h):
+            rows = pl.ds(pl.multiple_of(place * ts, ts), ts)
+
+            @pl.loop(0, hidden // wcol)
+            def _(c):
+                cols = pl.ds(pl.multiple_of(c * wcol, wcol), wcol)
+                value = nt(o_v[rows, :], w_v[cols, :])
+                own_v[rows, cols] = value
+                part_send[rows, cols] = value.astype(BF16)
+
+            k = len(part_copies)
+            copy = pltpu.make_async_remote_copy(
+                src_ref=part_send.at[rows],
+                dst_ref=part_recv.at[rows],
+                send_sem=part_ssem.at[k],
+                recv_sem=part_rsem.at[k],
+                device_id=dev(idx, 1 - core),
+                device_id_type=MESH,
+            )
+            copy.start()
+            part_copies.append(copy)
+
+    hid_done = []
+    hid_stores = []
+
+    def hid_part(h):
+        for place in shards_of(h):
+            k = len(hid_done)
+            hid_done.append(k)
+            part_copies[k].wait_recv()
+
+            @pl.loop(0, ts // gelu_rows)
+            def _(r):
+                start = place * ts + r * gelu_rows
+                rows = pl.ds(pl.multiple_of(start, gelu_rows), gelu_rows)
+
+                @pl.loop(0, hidden // col)
+                def _(c):
+                    cols = pl.ds(pl.multiple_of(c * col, col), col)
+                    total = own_v[rows, cols] + part_recv[rows, cols].astype(F32)
+                    hid_v[rows, cols] = (total * slope_v[rows, cols]).astype(BF16)
+
+            rows = pl.ds(pl.multiple_of(place * ts, ts), ts)
+            store = pltpu.make_async_copy(hid_v.at[rows], hid_out.at[rows], hid_sem.at[k])
+            store.start()
+            hid_stores.append(store)
 
     span = tokens // 2
     core_cols = pl.ds(pl.multiple_of(core * span, span), span)
@@ -218,6 +269,13 @@
                 s1_keep[k] = value
             else:
                 s1_send[k] = value.astype(BF16)
+
+    for k in range(n // 2):
+        gelu_part(k)
+    step(0, 1)
+    for k in range(n // 2, n):
+        gelu_part(k)
+    step(1, 1)
 
     s_rows(1 - b, False)
     s1 = pltpu.make_async_remote_copy(
@@ -230,38 +288,12 @@
     )
     s1.start()
     s_rows(b, True)
-
-    i_ticks = list(ticks)
-
-    def next_tick():
-        if i_ticks:
-            tick(1, *i_ticks.pop(0))
-
     w_copy.wait()
-    part_rows = tokens // CHUNKS
-    part_copies = []
-    for k in range(CHUNKS):
-        rows = pl.ds(k * part_rows, part_rows)
-        wcol = 512 if hidden % 512 == 0 else 128
-
-        @pl.loop(0, hidden // wcol)
-        def _(c):
-            cols = pl.ds(pl.multiple_of(c * wcol, wcol), wcol)
-            value = nt(o_v[rows, :], w_v[cols, :])
-            own_v[rows, cols] = value
-            part_send[rows, cols] = value.astype(BF16)
-
-        copy = pltpu.make_async_remote_copy(
-            src_ref=part_send.at[rows],
-            dst_ref=part_recv.at[rows],
-            send_sem=part_ssem.at[k],
-            recv_sem=part_rsem.at[k],
-            device_id=dev(idx, 1 - core),
-            device_id_type=MESH,
-        )
-        copy.start()
-        part_copies.append(copy)
-        next_tick()
+    o_own.wait()
+    part(0)
+    step(0, 2)
+    part(1)
+    hid_part(0)
 
     s1.wait()
 
@@ -284,24 +316,10 @@
         )
         copy.start()
         s2_copies.append(copy)
-
-    for k in range(CHUNKS):
-        part_copies[k].wait_recv()
-
-        @pl.loop(0, part_rows // gelu_rows)
-        def _(r):
-            rows = pl.ds(pl.multiple_of(k * part_rows + r * gelu_rows, gelu_rows), gelu_rows)
-
-            @pl.loop(0, hidden // col)
-            def _(c):
-                cols = pl.ds(pl.multiple_of(c * col, col), col)
-                total = own_v[rows, cols] + part_recv[rows, cols].astype(F32)
-                hid_v[rows, cols] = (total * slope_v[rows, cols]).astype(BF16)
-
-        if k % 2 == 1:
-            next_tick()
-    hid_store = pltpu.make_async_copy(hid_v, hid_out, local_sem.at[3])
-    hid_store.start()
+    step(1, 2)
+    part(2)
+    hid_part(1)
+    step(0, 3)
 
     for copy in s2_copies:
         copy.wait()
@@ -330,6 +348,9 @@
 
     act_store = pltpu.make_async_copy(act_t, act_out, local_sem.at[0])
     act_store.start()
+    step(1, 3)
+    part(3)
+    hid_part(2)
     for d in range(1, A):
         copy = s3_copies[d - 1]
         copy.wait_send()
@@ -364,55 +385,82 @@
         return copy, back
 
     copy, back = swap((core, b), (core, 1 - b), s4_sem, dev(partner))
-    next_tick()
+    for h in range(4, hops):
+        step(0, h)
+        part(h)
+        hid_part(h - 1)
+        step(1, h)
+    hid_part(hops - 1)
     copy.wait_send()
     back.wait_recv()
     copy, back = swap((core,), (1 - core,), s5_sem, dev(idx, 1 - core))
-    while i_ticks:
-        next_tick()
+    step(0, hops)
+    o_store = pltpu.make_async_copy(o_v, o_full, local_sem.at[1])
+    o_store.start()
+    part(hops)
     copy.wait_send()
     back.wait_recv()
     s_store = pltpu.make_async_copy(s_v, s_out, local_sem.at[4])
     s_store.start()
+    hid_part(hops)
+    step(1, hops)
     for copy in sent:
         copy.wait_send()
     for copy in part_copies:
         copy.wait_send()
     i_own.wait()
     o_store.wait()
-    hid_store.wait()
+    for store in hid_stores:
+        store.wait()
     act_store.wait()
     s_store.wait()
 
 
-def finish(act_t, hid, o_tile, i_tile, own, s, state, down, up, gram, left, s_keep, g_keep, sem):
+def finish(act_t, hid, o, i_tile, own, s, state, down, up, gram, left, keep, state_sem, gram_sem, whole_own=False):
     step = pl.program_id(0)
-    rows = own.shape[1]
-    tile = o_tile.shape[1]
+    rows = keep.shape[0]
+    tile = keep.shape[1] // STEPS
     cols = pl.ds(pl.multiple_of(step * tile, tile), tile)
+    load = pltpu.make_async_copy(state.at[:, 0, :], keep, state_sem)
 
     @pl.when(step == 0)
     def _():
-        copy = pltpu.make_async_copy(state.at[:, 0, :], s_keep, sem.at[0])
-        copy.start()
+        load.start()
+
+    down[...] = nn(act_t[...], o[...]).astype(BF16)
+    up[...] = tn(i_tile[...], hid[...]).astype(BF16)
+
+    @pl.when(step == 0)
+    def _():
         span = s.shape[2]
+        if whole_own:
+            mine = own[:, pl.ds(pl.multiple_of(lax.axis_index("inp") * rows, rows), rows)]
+        else:
+            mine = own[...]
         for c in range(2):
-            value = tn(own[...], s[c])
+            value = tn(mine, s[c])
             high = value.astype(BF16)
             left[0, :, c * span : (c + 1) * span] = high
             left[1, :, c * span : (c + 1) * span] = (value - high.astype(F32)).astype(BF16)
-        copy.wait()
-
-    down[...] = nn(act_t[...], o_tile[...]).astype(BF16)
-    up[...] = tn(i_tile[...], hid[...]).astype(BF16)
-    total = nn(left[0], o_tile[...]) + nn(left[1], o_tile[...])
-    g_keep[:, cols] = ema_decay * s_keep[:, cols] + (1.0 - ema_decay) * total
-
-    @pl.when(step == pl.num_programs(0) - 1)
+        load.wait()
+
+    total = nn(left[0], o[:, cols]) + nn(left[1], o[:, cols])
+    keep[:, cols] = ema_decay * keep[:, cols] + (1.0 - ema_decay) * total
+
+    def store(k):
+        part = pl.ds(k * tile, tile)
+        return pltpu.make_async_copy(keep.at[:, part], gram.at[:, 0, part], gram_sem.at[k])
+
+    for k in range(STEPS):
+
+        @pl.when(step == k)
+        def _():
+            store(k).start()
+
+    @pl.when(step == STEPS - 1)
     def _():
-        copy = pltpu.make_async_copy(g_keep, gram.at[:, 0, :], sem.at[1])
-        copy.start()
-        copy.wait()
+        for k in range(STEPS):
+            store(k).wait()
 
 
 def shards(n, inputs, pre_act, out_grad, w_down, gram_state):
@@ -456,8 +504,8 @@
             pltpu.VMEM((2, 2, A, ts, span), BF16),
             dma((2, 2, hops, 2)),
             dma((2, 2, hops, 2)),
-            dma((CHUNKS,)),
-            dma((CHUNKS,)),
+            dma((n,)),
+            dma((n,)),
             dma((2,)),
             dma((extra,)),
             dma((extra,)),
@@ -465,6 +513,7 @@
             dma((extra,)),
             dma((2,)),
             dma((2,)),
+            dma((n,)),
             dma((n,)),
             dma((5,)),
         ],
@@ -475,36 +524,38 @@
     )(inputs, pre_act, out_grad, w_down)
     s = s.reshape(2, tokens, span)
     rows = gram_state.shape[0]
-    own = lax.dynamic_slice_in_dim(o_full, lax.axis_index("inp") * rows, rows, 1)
-    tile = 256
-    keep = lambda i: (0, 0)
+    whole_own = rows % 128 == 0
+    own = o_full
+    if not whole_own:
+        own = lax.dynamic_slice_in_dim(o_full, lax.axis_index("inp") * rows, rows, 1)
+    fixed = lambda i: (0, 0)
     return pl.pallas_call(
-        finish,
-        grid=(width // tile,),
+        functools.partial(finish, whole_own=whole_own),
+        grid=(STEPS,),
         out_shape=(
             shape((hidden, width), BF16),
             shape((width, hidden), BF16),
             shape(gram_state.shape, F32),
         ),
         in_specs=[
-            pl.BlockSpec((hidden, tokens), keep),
-            pl.BlockSpec((tokens, hidden), keep),
-            pl.BlockSpec((tokens, tile), lambda i: (0, i)),
-            pl.BlockSpec((tokens, tile), lambda i: (0, i)),
-            pl.BlockSpec((tokens, rows), keep),
+            pl.BlockSpec((hidden // STEPS, tokens), lambda i: (i, 0)),
+            pl.BlockSpec((tokens, hidden), fixed),
+            pl.BlockSpec((tokens, width), fixed),
+            pl.BlockSpec((tokens, width // STEPS), lambda i: (0, i)),
+            pl.BlockSpec(own.shape, fixed),
             pl.BlockSpec((2, tokens, span), lambda i: (0, 0, 0)),
             any_spec,
         ],
         out_specs=(
-            pl.BlockSpec((hidden, tile), lambda i: (0, i)),
-            pl.BlockSpec((tile, hidden), lambda i: (i, 0)),
+            pl.BlockSpec((hidden // STEPS, width), lambda i: (i, 0)),
+            pl.BlockSpec((width // STEPS, hidden), lambda i: (i, 0)),
             any_spec,
         ),
         scratch_shapes=[
             pltpu.VMEM((2, rows, tokens), BF16),
             pltpu.VMEM((rows, width), F32),
-            pltpu.VMEM((rows, width), F32),
-            dma((2,)),
+            dma(()),
+            dma((STEPS,)),
         ],
         compiler_params=pltpu.CompilerParams(vmem_limit_bytes=56 * 1024 * 1024),
         name="finish",

time: 85.6 us -> 76.2 us (0.89)
  Pallas kernels: 82.8 us -> 74.7 us
  local copies, waits for them, and re-layouts: 1.68 us -> 0 us
    pallas_call x1, Pallas kernels: 66.2 us -> 59.4 us  [shards(): pl.pallas_call(functools.partial(exchange, n), out_shape=(shape((tokens,...]
    dynamic_slice x1 -> x0, local copies, waits for them, and re-layouts: 1.68 us -> none  [shards(): lax.dynamic_slice_in_dim(o_full, lax.axis_index('inp') * rows, rows, 1)]
    pallas_call x1, Pallas kernels: 16.6 us -> 15.3 us  [shards(): pl.pallas_call(functools.partial(finish, whole_own=whole_own), grid=(STEP...]
where the time goes in v3:
time: 76.2 us; the launch traced here: 75.3 us
  Pallas kernels  74.7 us (98%)
    pallas_call x1, Pallas kernels, shards(): pl.pallas_call(functools.partial(exchange, n), out_shape=(shape((tokens,...  59.4 us
    pallas_call x1, Pallas kernels, shards(): pl.pallas_call(functools.partial(finish, whole_own=whole_own), grid=(STEP...  15.3 us

profile of v3, /device:TPU:0, one launch (start us, length us, event | category | flops | bytes accessed | tf_op | source)
XLA Modules:
  0.0 75.3 jit_solution(7469162504385704410)
XLA Ops:
  0.6 59.4 %exchange.1 = (bf16[512,2048]{1,0:T(8,128)(2,1)}, bf16[512,2048]{1,0:T(8,128)(2,1)}, bf16[512,1536]{1,0:T(8,128)(2,1)}, bf16[1536,512]{1,0:T(8,128)(2,1)}, bf16[2,2,4,64,256]{4,3,2,1,0:T(8,128)(2,1)}) custom-call(bf16[64,2048]{1,0:T(8,128)(2,1)} %inputs.1, bf16[512,1536]{1,0:T(8,128)(2,1)} %pre_act.1, bf16[64,2048]{1,0:T(8,128)(2,1)} %out_grad.1, ...), custom_call_target="tpu_custom_call" | custom-call | tf_op jit(solution)/shard_map/exchange/pallas_call | solution.py:477
  60.0 15.3 %finish.1 = (bf16[1536,2048]{1,0:T(8,128)(2,1)}, bf16[2048,1536]{1,0:T(8,128)(2,1)}, f32[256,1,2048]{2,1,0:T(1,128)}) custom-call(bf16[1536,512]{1,0:T(8,128)(2,1)} %get-tuple-element.8.act_t, bf16[512,1536]{1,0:T(8,128)(2,1)} %get-tuple-element.9.hid, bf16[512,2048]{1,0:T(8,128)(2,1)} %get-tuple-element.10.o.own, ...), custom_call_target="tpu_custom_call" | custom-call | tf_op jit(solution)/shard_map/finish/pallas_call | solution.py:532
